TPU v7x, 32 devices: a whole 2x2x4 slice. The times are simulated.
32 devices in a mesh: frames: 8 (over z, y), heads: 4 (over x, core).
Axes of the slice: x: 2, y: 2, z: 4, core: 2. Of those that a mesh axis runs over, the one named last changes fastest.
Arguments:
- bank_query: bfloat16 [64, 64, 5120], P(None, 'frames', 'heads'), may hold values from -2048 to 2048
- char_bank: bfloat16 [2, 8, 768, 5120], P(None, None, 'frames', 'heads'), may hold values from -8 to 8
- char_slots: int32 [8, 2], replicated, may hold values from 0 to 7, as said below
- slot_live: int32 [8, 2], replicated, may hold values from 0 to 1, as said below
- frame_tokens: bfloat16 [3, 64, 64, 5120], P(None, None, 'frames', 'heads'), may hold values from -2048 to 2048
- out_weight: bfloat16 [5120, 5120], P('heads'), may hold values from -0.078125 to 0.078125
Outputs:
- blended: bfloat16 [64, 64, 5120], P('heads', 'frames')
Inputs may be any that keep to these rules, and one draw needn't show every extreme that they name: `char_slots`: the two ids of a shard differ. `slot_live`: slot 0 of every shard is 1.
All inputs are finite; a program needn't handle non-finite values.
Results may differ from a plain program's by a relative error of at most 0.014.
Values may be sent and summed in bfloat16 or wider, within the bound.
No kernel may reach another device: no remote copies, remote signals or barrier semaphores. Data moves between devices by JAX's collectives and lax.ppermute only.
A program may use at most 128 MiB of HBM per device.

v0:
```python
import jax
import jax.numpy as jnp
from jax import lax
from jax.sharding import PartitionSpec as P

HEAD_DIM = 128


def absorb(running, queries, key_rows, value_rows, slot_open):
    peak, totals, gathered = running
    scores = jnp.einsum(
        "qhd,khd->qhk", queries, key_rows, preferred_element_type=jnp.float32
    ) * HEAD_DIM ** (-0.5)
    new_peak = jnp.maximum(peak, jnp.max(scores, axis=-1))
    weights = jnp.exp(scores - new_peak[..., None])
    rescale = jnp.exp(peak - new_peak)
    new_totals = totals * rescale + jnp.sum(weights, axis=-1)
    new_gathered = gathered * rescale[..., None] + jnp.einsum(
        "qhk,khd->qhd", weights.astype(jnp.bfloat16), value_rows, preferred_element_type=jnp.float32
    )
    return (
        jnp.where(slot_open, new_peak, peak),
        jnp.where(slot_open, new_totals, totals),
        jnp.where(slot_open, new_gathered, gathered),
    )


def frame_attend(arrived):
    queries = arrived[0]
    key_rows = arrived[1]
    value_rows = arrived[2]
    scores = jnp.einsum(
        "sfhd,sghd->sfhg", queries, key_rows, preferred_element_type=jnp.float32
    ) * HEAD_DIM ** (-0.5)
    peak = jnp.max(scores, axis=-1, keepdims=True)
    weights = jnp.exp(scores - peak)
    totals = jnp.sum(weights, axis=-1, keepdims=True)
    attended = (
        jnp.einsum(
            "sfhg,sghd->sfhd",
            weights.astype(jnp.bfloat16),
            value_rows,
            preferred_element_type=jnp.float32,
        )
        / totals
    )
    attended = attended.astype(jnp.bfloat16)
    return lax.all_to_all(attended, "frames", split_axis=1, concat_axis=0, tiled=True)


def local(bank_query, char_bank, char_slots, slot_live, frame_tokens, out_weight):
    spatial, frames_here, local_width = bank_query.shape
    heads_here = local_width // HEAD_DIM
    row_total = spatial * frames_here
    queries = bank_query.reshape(row_total, heads_here, HEAD_DIM)
    shard_index = lax.axis_index("frames")
    opened = lax.dynamic_index_in_dim(slot_live, shard_index, 0, keepdims=False) > 0
    start_state = (
        jnp.full((row_total, heads_here), -1e30, jnp.float32),
        jnp.zeros((row_total, heads_here), jnp.float32),
        jnp.zeros((row_total, heads_here, HEAD_DIM), jnp.float32),
    )
    outgoing = jnp.take(char_bank, char_slots.T, axis=1)
    arrived = lax.all_to_all(outgoing, "frames", split_axis=2, concat_axis=3, tiled=True)
    running = start_state
    for slot_index in range(2):
        key_rows = arrived[0, slot_index, 0].reshape(-1, heads_here, HEAD_DIM)
        value_rows = arrived[1, slot_index, 0].reshape(-1, heads_here, HEAD_DIM)
        running = absorb(running, queries, key_rows, value_rows, opened[slot_index])
    peak, totals, gathered = running
    ref_out = gathered / totals[..., None]
    token_block = frame_tokens.reshape(3, spatial, frames_here, heads_here, HEAD_DIM)
    frame_out = frame_attend(
        lax.all_to_all(token_block, "frames", split_axis=1, concat_axis=2, tiled=True)
    )
    combined = (
        ref_out + frame_out.reshape(row_total, heads_here, HEAD_DIM).astype(jnp.float32)
    ).astype(jnp.bfloat16)
    combined = combined.reshape(row_total, local_width)
    head_count = lax.axis_size("heads")
    summed = lax.psum_scatter(
        jnp.dot(combined, out_weight, preferred_element_type=jnp.float32).astype(jnp.bfloat16),
        "heads",
        scatter_dimension=0,
        tiled=True,
    ).astype(jnp.float32)
    return summed.reshape(spatial // head_count, frames_here, -1).astype(jnp.bfloat16)


def solution(mesh):
    in_specs = (
        P(None, "frames", "heads"),
        P(None, None, "frames", "heads"),
        P(),
        P(),
        P(None, None, "frames", "heads"),
        P("heads", None),
    )
    out_specs = P("heads", "frames", None)
    return jax.shard_map(local, mesh=mesh, in_specs=in_specs, out_specs=out_specs, check_vma=False)
```

profile of v0, /device:TPU:0, one launch (start us, length us, event | category | flops | bytes accessed | tf_op | source)
XLA Modules:
  0.0 460.1 jit_solution(17884820856243157204)
XLA Ops:
  6.5 2.8 copy.84
  9.3 94.6 %all_to_all.36 = bf16[3,64,8,10,128]{4,2,3,0,1:T(8,128)(2,1)S(1)} all-to-all(bf16[3,64,8,10,128]{4,2,3,0,1:T(8,128)(2,1)S(1)} %copy.84), channel_id=1, replica_groups=mesh['frames'=8,'heads'=4] {'frames'}, dimensions={1} | all-to-all | bytes 7864320 | tf_op jit(solution)/shard_map/all_to_all | solution.py:74
  104.0 0.7 copy.85
  104.6 0.8 fusion.43
  105.4 0.8 bitcast_reduce_fusion.2
  106.3 0.7 fusion.21
  107.0 1.5 fusion.14
  108.5 0.0 copy-start.7
  108.5 1.9 copy.90
  110.4 3.6 all-to-all-start.2
  114.0 0.0 copy-done.7
  114.0 0.1 reshape.79
  114.1 6.7 %gather_fusion = bf16[16,2,96,1280]{3,2,1,0:T(8,128)(2,1)} fusion(bf16[2,8,96,1280]{3,2,1,0:T(8,128)(2,1)} %param.7, s32[1024]{0:T(1024)S(1)} %pad_clamp_fusion), kind=kCustom, calls=%fused_computation | custom fusion | bytes 15728704 | tf_op jit(solution)/shard_map/jit(_take)/gather | solution.py:63
  120.8 4.0 select_bitcast_fusion
  124.8 3.8 copy.72
  128.6 0.0 copy-start.6
  128.6 16.4 %all-to-all-done.2 = bf16[8,64,10,128]{3,0,2,1:T(8,128)(2,1)S(1)} async-done(((bf16[8,64,10,128]{3,0,2,1:T(8,128)(2,1)}), bf16[8,64,10,128]{3,0,2,1:T(8,128)(2,1)S(1)}, u32[]{:S(2)}, u32[]{:S(2)}) %all-to-all-start.2) | async-done | bytes 1310752 | tf_op jit(solution)/shard_map/all_to_all | solution.py:48
  145.0 4.9 %all-to-all-start = ((bf16[2,2,8,96,1280]{4,3,1,0,2:T(8,128)(2,1)}), bf16[2,2,8,96,1280]{4,3,1,0,2:T(8,128)(2,1)}, u32[]{:S(2)}, u32[]{:S(2)}) async-start(bf16[2,2,8,96,1280]{4,3,1,0,2:T(8,128)(2,1)} %copy.72), calls=%async_computation | async-start | bytes 15728640 | tf_op jit(solution)/shard_map/all_to_all | solution.py:64
  149.9 0.0 copy-start.8
  149.9 0.2 reduce-scatter.2.cloned.1.call-start
  150.2 0.0 copy-done.6
  150.2 1.8 reshape.72
  152.0 0.0 copy-done.8
  152.0 0.1 dynamic-slice_compare_fusion
  152.0 0.5 fusion.44
  152.6 0.3 convert_bitcast_fusion
  152.9 0.3 copy.92
  153.3 2.1 copy.93
  155.4 165.3 %all-to-all-done = bf16[2,2,8,96,1280]{4,3,1,0,2:T(8,128)(2,1)} async-done(((bf16[2,2,8,96,1280]{4,3,1,0,2:T(8,128)(2,1)}), bf16[2,2,8,96,1280]{4,3,1,0,2:T(8,128)(2,1)}, u32[]{:S(2)}, u32[]{:S(2)}) %all-to-all-start) | async-done | bytes 7864352 | tf_op jit(solution)/shard_map/all_to_all | solution.py:64
  320.7 3.8 copy.73
  324.6 2.6 fusion.42
  327.2 2.3 copy.74
  329.5 0.0 copy-start.1
  329.5 4.2 copy.79
  333.7 0.0 copy-done.1
  333.7 0.0 copy-start.3
  333.7 9.5 %bitcast_reduce_fusion.1 = (f32[512,10]{0,1:T(8,128)S(1)}, f32[10,768,512]{2,1,0:T(8,128)}) fusion(bf16[768,10,128]{0,2,1:T(8,128)(2,1)} %bitcast.105, bf16[512,10,128]{2,1,0:T(8,128)(2,1)S(1)} %copy-done.1), kind=kOutput, calls=%fused_computation.5 | convolution fusion | flops 1014492160 | bytes 19025920 | tf_op jit(solution)/shard_map/qhd,khd->qhk/dot_general | solution.py:11
  343.2 0.0 copy-done.3
  343.2 7.9 %bitcast_reduce_fusion = (f32[512,10]{0,1:T(8,128)S(1)}, f32[10,768,512]{2,1,0:T(8,128)}) fusion(bf16[768,10,128]{0,2,1:T(8,128)(2,1)S(1)} %bitcast.104, bf16[512,10,128]{2,1,0:T(8,128)(2,1)S(1)} %copy-done.1), kind=kOutput, calls=%fused_computation.2 | convolution fusion | flops 1014492160 | bytes 19025920 | tf_op jit(solution)/shard_map/qhd,khd->qhk/dot_general | solution.py:11
  351.1 0.0 copy-start.2
  351.1 4.2 copy.82
  355.3 0.0 copy-done.2
  355.3 2.4 copy.77
  357.6 0.6 exponential_multiply_fusion
  358.2 0.0 copy-start
  358.2 7.8 %fusion.6 = f32[10,128,512]{2,1,0:T(8,128)S(1)} fusion(bf16[768,10,128]{0,2,1:T(8,128)(2,1)} %bitcast.103, f32[10,768,512]{2,1,0:T(8,128)} %get-tuple-element.24, f32[512,10]{0,1:T(8,128)S(1)} %get-tuple-element.15), kind=kOutput, calls=%fused_computation.11 | convolution fusion | flops 1018429440 | bytes 20336640 | tf_op jit(solution)/shard_map/qhk,khd->qhd/dot_general | solution.py:18
  366.0 2.7 copy-done
  368.7 0.0 copy-start.4
  368.7 0.0 copy-start.5
  368.7 8.8 %fusion.2 = (f32[512,10]{0,1:T(8,128)S(1)}, f32[512,10]{0,1:T(8,128)S(1)}) fusion(f32[10,768,512]{2,1,0:T(8,128)} %get-tuple-element.22, f32[512,10]{0,1:T(8,128)S(1)} %get-tuple-element.16, f32[512,10]{0,1:T(8,128)S(1)} %get-tuple-element.15, f32[10,768,512]{2,1,0:T(8,128)S(1)} %copy-done), kind=kLoop, calls=%fused_computation.7 | loop fusion | flops 23582720 | bytes 31539200 | tf_op jit(solution)/shard_map/reduce_sum | solution.py:17
  377.6 1.2 add_select_fusion
  378.8 0.0 copy-done.4
  378.8 0.0 copy-done.5
  378.8 10.2 %fusion.20 = bf16[512,10,128]{0,2,1:T(8,128)(2,1)S(1)} fusion(f32[512,10,128]{0,2,1:T(8,128)S(1)} %copy-done.4, f32[10,128,512]{2,1,0:T(8,128)S(1)} %fusion.6, bf16[768,10,128]{0,2,1:T(8,128)(2,1)S(1)} %bitcast.107, f32[10,768,512]{2,1,0:T(8,128)} %get-tuple-element.22, f32[512,10]{0,1:T(8,128)S(1)} %get-tuple-element.16, ...), kind=kOutput, calls=%fused_computation.31 | convolution fusion | flops 1023672320 | bytes 24330242 | tf_op jit(solution)/shard_map/qhk,khd->qhd/dot_general | solution.py:18
  389.1 13.5 %convolution_convert_fusion = bf16[512,5120]{1,0:T(8,128)(2,1)} fusion(bf16[512,1280]{0,1:T(8,128)(2,1)S(1)} %bitcast.108, bf16[1280,5120]{1,0:T(8,128)(2,1)} %param.11), kind=kOutput, calls=%fused_computation.18 | convolution fusion | flops 6713507840 | bytes 19660800 | tf_op jit(solution)/shard_map/dot_general | solution.py:82
  402.6 0.0 reduce-scatter.2.cloned.1.call-update
  402.6 50.6 %reduce-scatter.2.cloned.1.call-done = bf16[128,5120]{1,0:T(8,128)(2,1)} async-done(((bf16[512,5120]{1,0:T(8,128)(2,1)}), bf16[128,5120]{1,0:T(8,128)(2,1)}) %reduce-scatter.2.cloned.1.call-update) | async-done | bytes 1310736 | tf_op jit(solution)/shard_map/reduce_scatter | solution.py:81
  (3 shorter events, 0.0 us)
Async XLA Ops:
  108.5 5.5 %copy-start.7 = (s32[8,2]{0,1:T(2,128)S(1)}, s32[8,2]{0,1:T(2,128)}, u32[]{:S(2)}) copy-start(s32[8,2]{0,1:T(2,128)} %param.8) | copy-start | bytes 196
  110.4 34.6 %all-to-all-start.2 = ((bf16[8,64,10,128]{3,0,2,1:T(8,128)(2,1)}), bf16[8,64,10,128]{3,0,2,1:T(8,128)(2,1)S(1)}, u32[]{:S(2)}, u32[]{:S(2)}) async-start(bf16[8,64,10,128]{3,0,2,1:T(8,128)(2,1)} %copy.90), calls=%async_computation.2 | async-start | bytes 2621440 | tf_op jit(solution)/shard_map/all_to_all | solution.py:48
  128.6 21.6 %copy-start.6 = (bf16[64,8,1280]{2,1,0:T(8,128)(2,1)S(1)}, bf16[64,8,1280]{2,1,0:T(8,128)(2,1)}, u32[]{:S(2)}) copy-start(bf16[64,8,1280]{2,1,0:T(8,128)(2,1)} %param.6) | copy-start | bytes 3932164
  145.0 175.7 %all-to-all-start = ((bf16[2,2,8,96,1280]{4,3,1,0,2:T(8,128)(2,1)}), bf16[2,2,8,96,1280]{4,3,1,0,2:T(8,128)(2,1)}, u32[]{:S(2)}, u32[]{:S(2)}) async-start(bf16[2,2,8,96,1280]{4,3,1,0,2:T(8,128)(2,1)} %copy.72), calls=%async_computation | async-start | bytes 15728640 | tf_op jit(solution)/shard_map/all_to_all | solution.py:64
  149.9 2.0 copy-start.8
  149.9 303.3 %reduce-scatter.2.cloned.1.call-start = ((), (), s32[]{:S(2)}) async-start(), calls=%async_computation.4 | async-start | bytes 6553600 | tf_op jit(solution)/shard_map/reduce_scatter | solution.py:81
  329.5 4.2 copy-start.1
  333.7 9.5 %copy-start.3 = (bf16[1,1,1,768,1280]{3,4,2,1,0:T(8,128)(2,1)S(1)}, bf16[1,1,1,768,1280]{3,4,2,1,0:T(8,128)(2,1)}, u32[]{:S(2)}) copy-start(bf16[1,1,1,768,1280]{3,4,2,1,0:T(8,128)(2,1)} %copy.79) | copy-start | bytes 5898244
  351.1 4.2 copy-start.2
  358.2 10.5 %copy-start = (f32[10,768,512]{2,1,0:T(8,128)S(1)}, f32[10,768,512]{2,1,0:T(8,128)}, u32[]{:S(2)}) copy-start(f32[10,768,512]{2,1,0:T(8,128)} %get-tuple-element.24) | copy-start | bytes 47185924
  368.7 10.1 %copy-start.4 = (f32[512,10,128]{0,2,1:T(8,128)S(1)}, f32[512,10,128]{0,2,1:T(8,128)}, u32[]{:S(2)}) copy-start(f32[512,10,128]{0,2,1:T(8,128)} %copy.93) | copy-start | bytes 7864324
  368.7 10.1 %copy-start.5 = (bf16[1,1,1,768,1280]{3,4,2,1,0:T(8,128)(2,1)S(1)}, bf16[1,1,1,768,1280]{3,4,2,1,0:T(8,128)(2,1)}, u32[]{:S(2)}) copy-start(bf16[1,1,1,768,1280]{3,4,2,1,0:T(8,128)(2,1)} %copy.77) | copy-start | bytes 5898244
Sparse Core Ops, SparseCore 0:
  402.7 50.4 reduce-scatter.1
where the time goes:
time: 461 us; the launch traced here: 460 us
  waiting for transfers between devices  232 us (50%)
  blocking collectives  94.6 us (21%)
  matrix products  51.3 us (11%)
  local copies, waits for them, and re-layouts  43.7 us (9%)
  other arithmetic  15.8 us (3%)
  between operations  13.6 us (3%)
  starting transfers between devices  8.72 us (2%)
    all_to_all x1, waiting for transfers between devices, local(): lax.all_to_all(outgoing, 'frames', split_axis=2, concat_axis=3, tiled=True)  165 us
    all_to_all x1, blocking collectives, local(): lax.all_to_all(token_block, 'frames', split_axis=1, concat_axis=2, tiled=...  94.6 us
    reduce_scatter x1, waiting for transfers between devices, local(): lax.psum_scatter(jnp.dot(combined, out_weight, preferred_element_type=jnp...  50.6 us
    dot_general x2, matrix products, absorb(): jnp.einsum('qhk,khd->qhd', weights.astype(jnp.bfloat16), value_rows, pref...  18 us
    dot_general x2, matrix products, absorb(): jnp.einsum('qhd,khd->qhk', queries, key_rows, preferred_element_type=jnp....  17.4 us
    all_to_all x1, waiting for transfers between devices, frame_attend(): lax.all_to_all(attended, 'frames', split_axis=1, concat_axis=0, tiled=True)  16.4 us
    dot_general x1, matrix products, local(): jnp.dot(combined, out_weight, preferred_element_type=jnp.float32)  13.5 us
  transfers between devices with their start and end apart: 3, of which 3 were waited for; matrix products, arithmetic and copies ran while one was open for 4% of the time, Pallas kernels for 0%

commit v1 on v0

v1 whole, which is shorter than its diff:
```python
import functools

import jax
import jax.numpy as jnp
from jax import lax
from jax.experimental import pallas as pl
from jax.experimental.pallas import tpu as pltpu
from jax.sharding import PartitionSpec as P

HEAD_DIM = 128
PARTS = 4


def softmax_over_rows(score_blocks):
    scale = HEAD_DIM ** (-0.5)
    peak = functools.reduce(
        jnp.maximum, [jnp.max(block, axis=0, keepdims=True) for block in score_blocks]
    )
    weights = [jnp.exp((block - peak) * scale) for block in score_blocks]
    totals = functools.reduce(
        jnp.add, [jnp.sum(block, axis=0, keepdims=True) for block in weights]
    )
    return weights, totals, peak * scale + jnp.log(totals)


def weighted(value_blocks, weights, totals):
    gathered = functools.reduce(
        jnp.add,
        [
            lax.dot_general(
                rows, block.astype(jnp.bfloat16), (((0,), (0,)), ((), ())),
                preferred_element_type=jnp.float32,
            )
            for rows, block in zip(value_blocks, weights)
        ],
    )
    return gathered * (1.0 / totals)


def attend_kernel(frames_here, slots_ref, live_ref, query_ref, bank_ref, frame_ref, ref_out, frame_out, stats_ref):
    head = pl.program_id(0)
    shards = query_ref.shape[0]
    rows = query_ref.shape[2]
    frame_keys = frame_ref.shape[1]
    key_spot = lax.broadcasted_iota(jnp.int32, (frame_keys, rows), 0) % rows // frames_here
    query_spot = lax.broadcasted_iota(jnp.int32, (frame_keys, rows), 1) // frames_here
    same_spot = key_spot == query_spot
    for shard in range(shards):
        queries = query_ref[shard, 0]
        blocks = []
        for slot in range(2):
            keys = bank_ref[0, slots_ref[shard, slot]]
            scores = lax.dot_general(
                keys, queries, (((1,), (1,)), ((), ())), preferred_element_type=jnp.float32
            )
            blocks.append(jnp.where(live_ref[shard, slot] > 0, scores, -jnp.inf))
        weights, totals, level = softmax_over_rows(blocks)
        values = [bank_ref[1, slots_ref[shard, slot]] for slot in range(2)]
        ref_out[shard] = weighted(values, weights, totals).astype(ref_out.dtype)
        stats_ref[shard, 0, pl.ds(head, 1), :] = level
        scores = lax.dot_general(
            frame_ref[0], query_ref[shard, 1], (((1,), (1,)), ((), ())),
            preferred_element_type=jnp.float32,
        )
        weights, totals, level = softmax_over_rows([jnp.where(same_spot, scores, -jnp.inf)])
        frame_out[shard] = weighted([frame_ref[1]], weights, totals).astype(frame_out.dtype)
        stats_ref[shard, 1, pl.ds(head, 1), :] = level


def attend(frames_here, slots, live, queries, bank, frame_kv):
    shards, _, rows, width = queries.shape
    heads = width // HEAD_DIM
    _, characters, tokens, _ = bank.shape
    frame_keys = frame_kv.shape[1]
    flops = 4 * shards * rows * width * (2 * tokens + frame_keys)
    return pl.pallas_call(
        functools.partial(attend_kernel, frames_here),
        grid=(heads,),
        in_specs=[
            pl.BlockSpec(memory_space=pltpu.SMEM),
            pl.BlockSpec(memory_space=pltpu.SMEM),
            pl.BlockSpec((shards, 2, rows, HEAD_DIM), lambda h: (0, 0, 0, h)),
            pl.BlockSpec((2, characters, tokens, HEAD_DIM), lambda h: (0, 0, 0, h)),
            pl.BlockSpec((2, frame_keys, HEAD_DIM), lambda h: (0, 0, h)),
        ],
        out_specs=[
            pl.BlockSpec((shards, HEAD_DIM, rows), lambda h: (0, h, 0)),
            pl.BlockSpec((shards, HEAD_DIM, rows), lambda h: (0, h, 0)),
            pl.BlockSpec((shards, 2, heads, rows), lambda h: (0, 0, 0, 0)),
        ],
        out_shape=[
            jax.ShapeDtypeStruct((shards, width, rows), jnp.bfloat16),
            jax.ShapeDtypeStruct((shards, width, rows), jnp.bfloat16),
            jax.ShapeDtypeStruct((shards, 2, heads, rows), jnp.float32),
        ],
        compiler_params=pltpu.CompilerParams(vmem_limit_bytes=32 * 1024 * 1024),
        cost_estimate=pl.CostEstimate(
            flops=4 * flops,
            bytes_accessed=2 * (queries.size + bank.size + frame_kv.size + queries.size),
            transcendentals=shards * rows * heads * (2 * tokens + frame_keys),
        ),
    )(slots, live, queries, bank, frame_kv)


def local(bank_query, char_bank, char_slots, slot_live, frame_tokens, out_weight):
    spatial, frames_here, width = bank_query.shape
    heads_here = width // HEAD_DIM
    head_groups = lax.axis_size("heads")
    shard_count = lax.axis_size("frames")
    across = 1 << ((shard_count.bit_length() - 1) // 2)
    along = shard_count // across
    lines = [[z * across + y for z in range(along)] for y in range(across)]
    column = lax.axis_index("frames") % across

    def mine(table):
        return lax.dynamic_index_in_dim(table.reshape(along, across, 2), column, 1, keepdims=False)

    slots, live = mine(char_slots), mine(slot_live)

    def from_plane(block):
        copies = [block]
        for step in range(1, across):
            pairs = [
                (z * across + y, z * across + (y + step) % across)
                for z in range(along)
                for y in range(across)
            ]
            copies.append(lax.ppermute(block, "frames", pairs))
        return copies

    parts = PARTS
    rows = spatial // parts * frames_here

    def part_of(block, part):
        lead = block.shape[:-3]
        cut = block.reshape(*lead, head_groups, parts, spatial // head_groups // parts, frames_here, width)
        return cut[..., part, :, :, :].reshape(*lead, rows, width)

    bank = jnp.concatenate(from_plane(char_bank), axis=2)
    pieces = []
    for part in range(parts):
        queries = jnp.stack([part_of(bank_query, part), part_of(frame_tokens[0], part)])
        queries = lax.all_gather(queries, "frames", axis_index_groups=lines)
        frame_kv = jnp.concatenate(from_plane(part_of(frame_tokens[1:], part)), axis=1)
        ref_part, frame_part, stats = attend(frames_here, slots, live, queries, bank, frame_kv)
        levels = lax.all_gather(stats, "frames", axis_index_groups=lines)
        peak = jnp.max(levels, axis=0)
        share = jnp.exp(stats - peak) / jnp.sum(jnp.exp(levels - peak), axis=0)
        share = share[:, :, :, None, :]
        split = (along, heads_here, HEAD_DIM, rows)
        summed = (
            ref_part.reshape(split).astype(jnp.float32) * share[:, 0]
            + frame_part.reshape(split).astype(jnp.float32) * share[:, 1]
        ).astype(jnp.bfloat16).reshape(along, width, rows)
        combined = lax.psum_scatter(
            summed, "frames", scatter_dimension=0, axis_index_groups=lines, tiled=False
        )
        projected = lax.dot_general(
            combined, out_weight, (((0,), (0,)), ((), ())), preferred_element_type=jnp.float32
        ).astype(jnp.bfloat16)
        pieces.append(lax.psum_scatter(projected, "heads", scatter_dimension=0, tiled=True))
    return jnp.concatenate(pieces, axis=0).reshape(spatial // head_groups, frames_here, -1)


def solution(mesh):
    in_specs = (
        P(None, "frames", "heads"),
        P(None, None, "frames", "heads"),
        P(),
        P(),
        P(None, None, "frames", "heads"),
        P("heads", None),
    )
    out_specs = P("heads", "frames", None)
    return jax.shard_map(local, mesh=mesh, in_specs=in_specs, out_specs=out_specs, check_vma=False)
```

time: 461 us -> 496 us (1.076)
  Pallas kernels: 0 us -> 65.1 us
  blocking collectives: 94.6 us -> 58.6 us
  waiting for transfers between devices: 232 us -> 258 us
  matrix products: 51.3 us -> 31.4 us
  other arithmetic: 15.8 us -> 21.1 us
  local copies, waits for them, and re-layouts: 43.7 us -> 38.6 us
    all_to_all x2 -> x0, waiting for transfers between devices: 182 us -> none  [the longest x1 165 us: local(): lax.all_to_all(outgoing, 'frames', split_axis=2, concat_axis=3, tiled=True)]
    ppermute x0 -> x5, waiting for transfers between devices: none -> 124 us  [from_plane(): copies.append(lax.ppermute(block, 'frames', pairs))]
    all_to_all x1 -> x0, blocking collectives: 94.6 us -> none  [local(): lax.all_to_all(token_block, 'frames', split_axis=1, concat_axis=2, tiled=...]
    reduce_scatter x1 -> x8, waiting for transfers between devices: 50.6 us -> 133 us  [the longest x4 107 us: local(): lax.psum_scatter(projected, 'heads', scatter_dimension=0, tiled=True)]
    pallas_call x0 -> x4, Pallas kernels: none -> 65.1 us  [attend(): pl.pallas_call(functools.partial(attend_kernel, frames_here), grid=(heads...]
    all_gather x0 -> x4, blocking collectives: none -> 58.6 us  [local(): levels = lax.all_gather(stats, 'frames', axis_index_groups=lines)]
    unnamed x18 -> x33, local copies, waits for them, and re-layouts: 2.74 us -> 31.1 us
    dot_general x7 -> x4, matrix products: 51.3 us -> 31.4 us  [local(): lax.dot_general(combined, out_weight, (((0,), (0,)), ((), ())), preferred...]
  transfers between devices with their start and end apart: 3 -> 17, of which waited for: 3 -> 10; matrix products, arithmetic and copies ran while one was open for 4% -> 11% of each run, Pallas kernels for 0% -> 13%
where the time goes in v1:
time: 496 us; the launch traced here: 495 us
  waiting for transfers between devices  258 us (52%)
  Pallas kernels  65.1 us (13%)
  blocking collectives  58.6 us (12%)
  local copies, waits for them, and re-layouts  38.6 us (8%)
  matrix products  31.4 us (6%)
  other arithmetic  21.1 us (4%)
  between operations  13.8 us (3%)
  starting transfers between devices  8.37 us (2%)
    ppermute x5, waiting for transfers between devices, from_plane(): copies.append(lax.ppermute(block, 'frames', pairs))  124 us
    reduce_scatter x4, waiting for transfers between devices, local(): lax.psum_scatter(projected, 'heads', scatter_dimension=0, tiled=True)  107 us
    pallas_call x4, Pallas kernels, attend(): pl.pallas_call(functools.partial(attend_kernel, frames_here), grid=(heads...  65.1 us
    all_gather x4, blocking collectives, local(): levels = lax.all_gather(stats, 'frames', axis_index_groups=lines)  58.6 us
    dot_general x4, matrix products, local(): lax.dot_general(combined, out_weight, (((0,), (0,)), ((), ())), preferred...  31.4 us
    unnamed x33, local copies, waits for them, and re-layouts  31.1 us
    reduce_scatter x4, waiting for transfers between devices, local(): lax.psum_scatter(summed, 'frames', scatter_dimension=0, axis_index_groups...  26.1 us
  transfers between devices with their start and end apart: 17, of which 10 were waited for; matrix products, arithmetic and copies ran while one was open for 11% of the time, Pallas kernels for 13%

profile of v1, /device:TPU:0, one launch (start us, length us, event | category | flops | bytes accessed | tf_op | source)
XLA Modules:
  0.0 495.0 jit_solution(12681240002554643562)
XLA Ops:
  6.5 1.3 slice-done
  8.0 0.3 copy-done.13
  8.3 0.9 pad_maximum_fusion.7
  9.3 0.9 pad_maximum_fusion.6
  10.3 0.9 pad_maximum_fusion.5
  11.2 3.0 collective-permute-start
  14.3 0.9 pad_maximum_fusion.4
  15.3 1.7 slice-done.1
  16.9 1.3 fusion.20
  18.5 0.1 copy.91
  18.8 2.6 constant_dynamic-update-slice_fusion.1
  21.4 92.1 %collective-permute-done.4 = bf16[2,128,1280]{2,1,0:T(8,128)(2,1)S(1)} collective-permute-done((bf16[2,128,1280]{2,1,0:T(8,128)(2,1)}, bf16[2,128,1280]{2,1,0:T(8,128)(2,1)S(1)}, u32[]{:S(2)}, u32[]{:S(2)}) %collective-permute-start.4) | collective-permute-done | bytes 655392 | tf_op jit(solution)/shard_map/ppermute | solution.py:128
  113.5 2.2 pad_maximum_fusion.3.frame_ref
  115.7 2.4 constant_dynamic-update-slice_fusion.bank_ref
  118.1 3.0 copy-done
  121.2 3.2 copy-done.1
  124.4 1.3 copy-done.5
  125.7 1.7 copy-done.12
  127.5 16.3 %shard_map.67 = (bf16[4,1280,128]{2,1,0:T(8,128)(2,1)S(1)}, bf16[4,1280,128]{2,1,0:T(8,128)(2,1)S(1)}, f32[4,2,10,128]{3,2,1,0:T(8,128)S(1)}) custom-call(s32[4,2]{1,0:T(4,128)S(1)} %bitcast.135, s32[4,2]{1,0:T(4,128)S(1)} %bitcast.139, bf16[4,2,128,1280]{3,2,1,0:T(8,128)(2,1)S(1)} %bitcast.146, bf16[2,8,192,1280]{3,2,1,0:T(8,128)(2,1)S(1)} %copy-done.1, ...), custom_call_target="tpu_custom_call" | custom-call | flops 6710886400 | bytes 14417920 | tf_op jit(solution)/shard_map/pallas_call | solution.py:76
  143.8 14.9 %all-gather.7 = f32[16,2,10,128]{3,1,2,0:T(2,128)S(1)} all-gather(f32[4,2,10,128]{3,1,2,0:T(2,128)S(1)} %copy.88), channel_id=9, replica_groups={{0,8,16,24},{4,12,20,28},{1,9,17,25},{5,13,21,29},{2,10,18,26},{6,14,22..., dimensions={0}, use_global_device_ids=true | all-gather | bytes 204800 | tf_op jit(solution)/shard_map/all_gather | solution.py:146
  158.7 0.1 exponential_reduce_fusion
  158.9 1.6 fusion.1
  160.6 1.6 collective-permute-start.3
  162.2 13.2 %collective-permute-done.3 = bf16[2,128,1280]{2,1,0:T(8,128)(2,1)S(1)} collective-permute-done((bf16[2,128,1280]{2,1,0:T(8,128)(2,1)}, bf16[2,128,1280]{2,1,0:T(8,128)(2,1)S(1)}, u32[]{:S(2)}, u32[]{:S(2)}) %collective-permute-start.3) | collective-permute-done | bytes 655392 | tf_op jit(solution)/shard_map/ppermute | solution.py:128
  175.3 2.2 pad_maximum_fusion.2.frame_ref
  177.6 3.2 copy-done.2
  180.8 1.3 copy-done.7
  182.1 1.7 copy-done.11
  183.9 16.3 %shard_map.66 = (bf16[4,1280,128]{2,1,0:T(8,128)(2,1)S(1)}, bf16[4,1280,128]{2,1,0:T(8,128)(2,1)S(1)}, f32[4,2,10,128]{3,2,1,0:T(8,128)S(1)}) custom-call(s32[4,2]{1,0:T(4,128)S(1)} %bitcast.136, s32[4,2]{1,0:T(4,128)S(1)} %bitcast.140, bf16[4,2,128,1280]{3,2,1,0:T(8,128)(2,1)S(1)} %bitcast.145, bf16[2,8,192,1280]{3,2,1,0:T(8,128)(2,1)S(1)} %copy-done.2, ...), custom_call_target="tpu_custom_call" | custom-call | flops 6710886400 | bytes 14417920 | tf_op jit(solution)/shard_map/pallas_call | solution.py:76
  200.2 14.5 %all-gather.5 = f32[16,2,10,128]{3,1,2,0:T(2,128)S(1)} all-gather(f32[4,2,10,128]{3,1,2,0:T(2,128)S(1)} %copy.80), channel_id=7, replica_groups={{0,8,16,24},{4,12,20,28},{1,9,17,25},{5,13,21,29},{2,10,18,26},{6,14,22..., dimensions={0}, use_global_device_ids=true | all-gather | bytes 204800 | tf_op jit(solution)/shard_map/all_gather | solution.py:146
  214.8 0.1 exponential_reduce_fusion.1
  214.9 1.6 fusion.3
  216.6 1.6 collective-permute-start.2
  218.2 9.8 %collective-permute-done.2 = bf16[2,128,1280]{2,1,0:T(8,128)(2,1)S(1)} collective-permute-done((bf16[2,128,1280]{2,1,0:T(8,128)(2,1)}, bf16[2,128,1280]{2,1,0:T(8,128)(2,1)S(1)}, u32[]{:S(2)}, u32[]{:S(2)}) %collective-permute-start.2) | collective-permute-done | bytes 655392 | tf_op jit(solution)/shard_map/ppermute | solution.py:128
  227.9 2.3 pad_maximum_fusion.1.frame_ref
  230.2 3.2 copy-done.3
  233.5 1.3 copy-done.8
  234.8 1.7 copy-done.10
  236.5 16.3 %shard_map.65 = (bf16[4,1280,128]{2,1,0:T(8,128)(2,1)S(1)}, bf16[4,1280,128]{2,1,0:T(8,128)(2,1)S(1)}, f32[4,2,10,128]{3,2,1,0:T(8,128)S(1)}) custom-call(s32[4,2]{1,0:T(4,128)S(1)} %bitcast.137, s32[4,2]{1,0:T(4,128)S(1)} %bitcast.141, bf16[4,2,128,1280]{3,2,1,0:T(8,128)(2,1)S(1)} %bitcast.144, bf16[2,8,192,1280]{3,2,1,0:T(8,128)(2,1)S(1)} %copy-done.3, ...), custom_call_target="tpu_custom_call" | custom-call | flops 6710886400 | bytes 14417920 | tf_op jit(solution)/shard_map/pallas_call | solution.py:76
  252.8 15.2 %all-gather.3 = f32[16,2,10,128]{3,1,2,0:T(2,128)S(1)} all-gather(f32[4,2,10,128]{3,1,2,0:T(2,128)S(1)} %copy.72), channel_id=5, replica_groups={{0,8,16,24},{4,12,20,28},{1,9,17,25},{5,13,21,29},{2,10,18,26},{6,14,22..., dimensions={0}, use_global_device_ids=true | all-gather | bytes 204800 | tf_op jit(solution)/shard_map/all_gather | solution.py:146
  268.1 0.1 exponential_reduce_fusion.2
  268.3 1.6 fusion.5
  269.9 1.5 collective-permute-start.1
  271.4 9.1 %collective-permute-done.1 = bf16[2,128,1280]{2,1,0:T(8,128)(2,1)S(1)} collective-permute-done((bf16[2,128,1280]{2,1,0:T(8,128)(2,1)S(1)}, bf16[2,128,1280]{2,1,0:T(8,128)(2,1)S(1)}, u32[]{:S(2)}, u32[]{:S(2)}) %collective-permute-start.1) | collective-permute-done | bytes 655392 | tf_op jit(solution)/shard_map/ppermute | solution.py:128
  280.6 1.2 pad_maximum_fusion.frame_ref
  281.8 3.2 copy-done.4
  285.0 1.3 copy-done.6
  286.4 1.8 copy-done.9
  288.1 16.3 %shard_map.64 = (bf16[4,1280,128]{2,1,0:T(8,128)(2,1)S(1)}, bf16[4,1280,128]{2,1,0:T(8,128)(2,1)S(1)}, f32[4,2,10,128]{3,2,1,0:T(8,128)S(1)}) custom-call(s32[4,2]{1,0:T(4,128)S(1)} %bitcast.138, s32[4,2]{1,0:T(4,128)S(1)} %bitcast.142, bf16[4,2,128,1280]{3,2,1,0:T(8,128)(2,1)S(1)} %bitcast.143, bf16[2,8,192,1280]{3,2,1,0:T(8,128)(2,1)S(1)} %copy-done.4, ...), custom_call_target="tpu_custom_call" | custom-call | flops 6710886400 | bytes 14417920 | tf_op jit(solution)/shard_map/pallas_call | solution.py:76
  304.4 14.0 %all-gather.1 = f32[16,2,10,128]{3,1,2,0:T(2,128)S(1)} all-gather(f32[4,2,10,128]{3,1,2,0:T(2,128)S(1)} %copy.64), channel_id=3, replica_groups={{0,8,16,24},{4,12,20,28},{1,9,17,25},{5,13,21,29},{2,10,18,26},{6,14,22..., dimensions={0}, use_global_device_ids=true | all-gather | bytes 204800 | tf_op jit(solution)/shard_map/all_gather | solution.py:146
  318.5 0.1 exponential_reduce_fusion.3
  318.6 1.6 fusion.7
  320.3 0.2 reduce-scatter.23.cloned.1.call-start
  320.6 7.9 %convolution_convert_fusion = bf16[128,5120]{1,0:T(8,128)(2,1)} fusion(bf16[1280,5120]{1,0:T(8,128)(2,1)} %param.11, bf16[1,1280,128]{2,1,0:T(8,128)(2,1)} %reduce-scatter.21.cloned.1.call-done), kind=kOutput, calls=%fused_computation | convolution fusion | flops 1678376960 | bytes 14745600 | tf_op jit(solution)/shard_map/dot_general | solution.py:158
  328.5 7.9 %convolution_convert_fusion.1 = bf16[128,5120]{1,0:T(8,128)(2,1)} fusion(bf16[1280,5120]{1,0:T(8,128)(2,1)} %param.11, bf16[1,1280,128]{2,1,0:T(8,128)(2,1)} %reduce-scatter.17.cloned.1.call-done), kind=kOutput, calls=%fused_computation.1 | convolution fusion | flops 1678376960 | bytes 14745600 | tf_op jit(solution)/shard_map/dot_general | solution.py:158
  336.5 1.6 reduce-scatter.13.cloned.1.call-done
  338.1 7.8 %convolution_convert_fusion.2 = bf16[128,5120]{1,0:T(8,128)(2,1)} fusion(bf16[1280,5120]{1,0:T(8,128)(2,1)} %param.11, bf16[1,1280,128]{2,1,0:T(8,128)(2,1)} %reduce-scatter.13.cloned.1.call-done), kind=kOutput, calls=%fused_computation.2 | convolution fusion | flops 1678376960 | bytes 14745600 | tf_op jit(solution)/shard_map/dot_general | solution.py:158
  346.0 24.5 %reduce-scatter.9.cloned.1.call-done = bf16[1,1280,128]{2,1,0:T(8,128)(2,1)} async-done(((bf16[4,1280,128]{2,1,0:T(8,128)(2,1)}), bf16[1,1280,128]{2,1,0:T(8,128)(2,1)}) %reduce-scatter.9.cloned.1.call-update) | async-done | bytes 327696 | tf_op jit(solution)/shard_map/reduce_scatter | solution.py:155
  370.4 7.8 %convolution_convert_fusion.3 = bf16[128,5120]{1,0:T(8,128)(2,1)} fusion(bf16[1280,5120]{1,0:T(8,128)(2,1)} %param.11, bf16[1,1280,128]{2,1,0:T(8,128)(2,1)} %reduce-scatter.9.cloned.1.call-done), kind=kOutput, calls=%fused_computation.3 | convolution fusion | flops 1678376960 | bytes 14745600 | tf_op jit(solution)/shard_map/dot_general | solution.py:158
  378.3 20.0 %reduce-scatter.23.cloned.1.call-done = bf16[32,5120]{1,0:T(8,128)(2,1)} async-done(((bf16[128,5120]{1,0:T(8,128)(2,1)}), bf16[32,5120]{1,0:T(8,128)(2,1)}) %reduce-scatter.23.cloned.1.call-update) | async-done | bytes 327696 | tf_op jit(solution)/shard_map/reduce_scatter | solution.py:161
  398.3 29.1 %reduce-scatter.19.cloned.1.call-done = bf16[32,5120]{1,0:T(8,128)(2,1)} async-done(((bf16[128,5120]{1,0:T(8,128)(2,1)}), bf16[32,5120]{1,0:T(8,128)(2,1)}) %reduce-scatter.19.cloned.1.call-update) | async-done | bytes 327696 | tf_op jit(solution)/shard_map/reduce_scatter | solution.py:161
  427.5 29.1 %reduce-scatter.15.cloned.1.call-done = bf16[32,5120]{1,0:T(8,128)(2,1)} async-done(((bf16[128,5120]{1,0:T(8,128)(2,1)}), bf16[32,5120]{1,0:T(8,128)(2,1)}) %reduce-scatter.15.cloned.1.call-update) | async-done | bytes 327696 | tf_op jit(solution)/shard_map/reduce_scatter | solution.py:161
  456.6 29.1 %reduce-scatter.11.cloned.1.call-done = bf16[32,5120]{1,0:T(8,128)(2,1)} async-done(((bf16[128,5120]{1,0:T(8,128)(2,1)}), bf16[32,5120]{1,0:T(8,128)(2,1)}) %reduce-scatter.11.cloned.1.call-update) | async-done | bytes 327696 | tf_op jit(solution)/shard_map/reduce_scatter | solution.py:161
  485.7 2.4 maximum_bitcast_fusion
  (73 shorter events, 1.7 us)
Async XLA Ops:
  6.5 1.3 slice-start
  6.5 114.6 %all-gather.19.cloned.1.call-start = ((), (), s32[]{:S(2)}) async-start(), calls=%async_computation.19 | async-start | bytes 3276800 | tf_op jit(solution)/shard_map/all_gather | solution.py:143
  6.5 1.7 copy-start.13
  9.2 168.3 %all-gather.17.cloned.1.call-start = ((), (), s32[]{:S(2)}) async-start(), calls=%async_computation.18 | async-start | bytes 3276800 | tf_op jit(solution)/shard_map/all_gather | solution.py:143
  10.2 220.0 %all-gather.15.cloned.1.call-start = ((), (), s32[]{:S(2)}) async-start(), calls=%async_computation.17 | async-start | bytes 3276800 | tf_op jit(solution)/shard_map/all_gather | solution.py:143
  11.2 270.6 %all-gather.13.cloned.1.call-start = ((), (), s32[]{:S(2)}) async-start(), calls=%async_computation.16 | async-start | bytes 3276800 | tf_op jit(solution)/shard_map/all_gather | solution.py:143
  11.2 104.5 %collective-permute-start = (bf16[2,8,96,1280]{3,2,1,0:T(8,128)(2,1)}, bf16[2,8,96,1280]{3,2,1,0:T(8,128)(2,1)}, u32[]{:S(2)}, u32[]{:S(2)}) collective-permute-start(bf16[2,8,96,1280]{3,2,1,0:T(8,128)(2,1)} %param.7), channel_id=1, source_target_pairs={{0,4},{4,0},{8,12},{12,8},{16,20},{20,16},{24,28},{28,24},{1,5},{5... | collective-permute-start | bytes 11796488 | tf_op jit(solution)/shard_map/ppermute | solution.py:128
  15.2 1.7 slice-start.1
  15.2 305.3 %reduce-scatter.21.cloned.1.call-start = ((), (), s32[]{:S(2)}) async-start(), calls=%async_computation.14 | async-start | bytes 1638400 | tf_op jit(solution)/shard_map/reduce_scatter | solution.py:155
  16.9 1.4 copy-start.14
  16.9 1.4 copy-start.15
  18.3 95.2 %collective-permute-start.4 = (bf16[2,128,1280]{2,1,0:T(8,128)(2,1)}, bf16[2,128,1280]{2,1,0:T(8,128)(2,1)S(1)}, u32[]{:S(2)}, u32[]{:S(2)}) collective-permute-start(bf16[2,128,1280]{2,1,0:T(8,128)(2,1)} %bitcast.39), channel_id=1, source_target_pairs={{0,4},{4,0},{8,12},{12,8},{16,20},{20,16},{24,28},{28,24},{1,5},{5... | collective-permute-start | bytes 1966088 | tf_op jit(solution)/shard_map/ppermute | solution.py:128
  118.1 3.1 copy-start
  121.2 3.2 copy-start.1
  124.4 1.3 copy-start.5
  125.7 1.7 copy-start.12
  160.5 168.0 %reduce-scatter.17.cloned.1.call-start = ((), (), s32[]{:S(2)}) async-start(), calls=%async_computation.12 | async-start | bytes 1638400 | tf_op jit(solution)/shard_map/reduce_scatter | solution.py:155
  160.6 14.8 %collective-permute-start.3 = (bf16[2,128,1280]{2,1,0:T(8,128)(2,1)}, bf16[2,128,1280]{2,1,0:T(8,128)(2,1)S(1)}, u32[]{:S(2)}, u32[]{:S(2)}) collective-permute-start(bf16[2,128,1280]{2,1,0:T(8,128)(2,1)} %bitcast.153), channel_id=1, source_target_pairs={{0,4},{4,0},{8,12},{12,8},{16,20},{20,16},{24,28},{28,24},{1,5},{5... | collective-permute-start | bytes 1966088 | tf_op jit(solution)/shard_map/ppermute | solution.py:128
  177.6 3.2 copy-start.2
  180.8 1.3 copy-start.7
  182.1 1.7 copy-start.11
  216.5 121.5 %reduce-scatter.13.cloned.1.call-start = ((), (), s32[]{:S(2)}) async-start(), calls=%async_computation.10 | async-start | bytes 1638400 | tf_op jit(solution)/shard_map/reduce_scatter | solution.py:155
  216.6 11.4 %collective-permute-start.2 = (bf16[2,128,1280]{2,1,0:T(8,128)(2,1)}, bf16[2,128,1280]{2,1,0:T(8,128)(2,1)S(1)}, u32[]{:S(2)}, u32[]{:S(2)}) collective-permute-start(bf16[2,128,1280]{2,1,0:T(8,128)(2,1)} %bitcast.151), channel_id=1, source_target_pairs={{0,4},{4,0},{8,12},{12,8},{16,20},{20,16},{24,28},{28,24},{1,5},{5... | collective-permute-start | bytes 1966088 | tf_op jit(solution)/shard_map/ppermute | solution.py:128
  230.2 3.2 copy-start.3
  233.4 1.3 copy-start.8
  234.8 1.7 copy-start.10
  269.9 100.6 %reduce-scatter.9.cloned.1.call-start = ((), (), s32[]{:S(2)}) async-start(), calls=%async_computation.8 | async-start | bytes 1638400 | tf_op jit(solution)/shard_map/reduce_scatter | solution.py:155
  269.9 10.7 %collective-permute-start.1 = (bf16[2,128,1280]{2,1,0:T(8,128)(2,1)S(1)}, bf16[2,128,1280]{2,1,0:T(8,128)(2,1)S(1)}, u32[]{:S(2)}, u32[]{:S(2)}) collective-permute-start(bf16[2,128,1280]{2,1,0:T(8,128)(2,1)S(1)} %bitcast.149), channel_id=1, source_target_pairs={{0,4},{4,0},{8,12},{12,8},{16,20},{20,16},{24,28},{28,24},{1,5},{5... | collective-permute-start | bytes 1966088 | tf_op jit(solution)/shard_map/ppermute | solution.py:128
  281.8 3.2 copy-start.4
  285.0 1.3 copy-start.6
  286.4 1.8 copy-start.9
  320.3 78.0 %reduce-scatter.23.cloned.1.call-start = ((), (), s32[]{:S(2)}) async-start(), calls=%async_computation.15 | async-start | bytes 1638400 | tf_op jit(solution)/shard_map/reduce_scatter | solution.py:161
  328.5 99.0 %reduce-scatter.19.cloned.1.call-start = ((), (), s32[]{:S(2)}) async-start(), calls=%async_computation.13 | async-start | bytes 1638400 | tf_op jit(solution)/shard_map/reduce_scatter | solution.py:161
  336.5 120.1 %reduce-scatter.15.cloned.1.call-start = ((), (), s32[]{:S(2)}) async-start(), calls=%async_computation.11 | async-start | bytes 1638400 | tf_op jit(solution)/shard_map/reduce_scatter | solution.py:161
  345.9 139.8 %reduce-scatter.11.cloned.1.call-start = ((), (), s32[]{:S(2)}) async-start(), calls=%async_computation.9 | async-start | bytes 1638400 | tf_op jit(solution)/shard_map/reduce_scatter | solution.py:161
Sparse Core Ops, SparseCore 0:
  9.4 57.4 all-gather.18
  68.5 53.5 all-gather.16
  123.7 56.1 all-gather.14
  181.3 56.0 all-gather.12
  239.5 32.6 reduce-scatter.20
  274.3 30.9 reduce-scatter.16
  307.6 30.3 reduce-scatter.12
  340.4 30.0 reduce-scatter.8
  373.0 25.3 reduce-scatter.22
  400.9 26.5 reduce-scatter.18
  430.0 26.5 reduce-scatter.14
  459.1 26.5 reduce-scatter.10
